TPU v7x, 32 devices: a whole 2x2x4 slice. The times are simulated.
32 devices in a mesh: rep: 4 (over z), gx: 4 (over x, core), gy: 2 (over y).
Axes of the slice: x: 2, y: 2, z: 4, core: 2. Of those that a mesh axis runs over, the one named last changes fastest.
Arguments:
- velocity: bfloat16 [4, 128, 64, 128], P('rep', 'gx', 'gy'), may hold values from -1.5 to 1.5
- tracers: bfloat16 [4, 128, 64, 128], P('rep', 'gx', 'gy'), may hold values from 0.5 to 2
- forcing: bfloat16 [12, 128, 64, 128], P('rep', 'gx', 'gy'), may hold values from -6 to 6
- coefficients: float32 [12], P('rep'), may hold values from -1.2 to 1.2
- land_mask: int32 [128, 64], P('gx', 'gy'), may hold values 0 or 1
- step_levels: int32 [3], replicated, may hold values from 0 to 3
Outputs:
- combined: float32 [128, 64, 128], P(('gx', 'rep'), 'gy')
- adjoints: float32 [12, 128, 64, 128], P('rep', 'gx', 'gy')
Inputs may be any that keep to these rules, and one draw needn't show every extreme that they name: `step_levels`: each entry names the group along rep that stores the level.
All inputs are finite; a program needn't handle non-finite values. No bound on the sum of `land_mask` on one device may be relied on, other than what follows from the above.
Results may differ from a plain program's by a relative error of at most 0.0003.
Values may be sent and summed in bfloat16 or wider, within the bound.
A program may use at most 64 MiB of HBM per device.

v0:
```python
import jax
import jax.numpy as jnp
from jax import lax
from jax.sharding import PartitionSpec as P

STEPS = 3


time_step = 0.1


def extended(cells, sides, width):
    for axis, dim in sides:
        count = lax.axis_size(axis)
        ends = count - 1
        head = lax.slice_in_dim(cells, 0, width, axis=dim)
        tail = lax.slice_in_dim(cells, cells.shape[dim] - width, cells.shape[dim], axis=dim)
        cells = jnp.concatenate(
            [
                lax.ppermute(tail, axis, [(i, (i + 1) % count) for i in range(ends)]),
                cells,
                lax.ppermute(head, axis, [((i + 1) % count, i) for i in range(ends)]),
            ],
            axis=dim,
        )
    return cells


def spread_2(x, axis, root):
    mine = lax.axis_index(axis) == root
    return lax.psum(jnp.where(mine, x, jnp.zeros_like(x)), axis)


def advance(state, speed_ext, tracer, ocean):
    half = state.shape[-1] // 2
    padded = extended(state, (("gx", 1), ("gy", 2)), 1)
    speed = speed_ext.astype(jnp.float32)
    along_x = jnp.concatenate([speed[..., :half], speed[..., :half]], axis=-1)[None]
    along_y = jnp.concatenate([speed[..., half:], speed[..., half:]], axis=-1)[None]
    east = along_x * padded
    north = along_y * padded
    advect = 0.5 * (east[:, :-2, 1:-1] - east[:, 2:, 1:-1]) + 0.5 * (
        north[:, 1:-1, :-2] - north[:, 1:-1, 2:]
    )
    spread = (
        padded[:, :-2, 1:-1]
        + padded[:, 2:, 1:-1]
        + padded[:, 1:-1, :-2]
        + padded[:, 1:-1, 2:]
        - 4.0 * state
    )
    tracer_f = tracer.astype(jnp.float32)[None]
    mixing = tracer_f[..., :half] * state[..., :half] - tracer_f[..., half:] * state[..., half:]
    exchange = jnp.concatenate([-mixing, mixing], axis=-1)
    return ocean * (state + time_step * (advect + spread + exchange))


def local(velocity, tracers, forcing, coefficients, land_mask, step_levels):
    ocean = land_mask.astype(jnp.float32)[None, :, :, None]
    state = forcing.astype(jnp.float32)
    own_speed = velocity[0]
    own_tracer = tracers[0]
    for step in range(STEPS):
        owner = step_levels[step]
        speed, tracer = (spread_2(own_speed, "rep", owner), spread_2(own_tracer, "rep", owner))
        speed_ext = extended(speed, (("gx", 0), ("gy", 1)), 1)
        state = advance(state, speed_ext, tracer, ocean)
    weighted = jnp.sum(coefficients[:, None, None, None] * state, axis=0)
    return (lax.psum_scatter(weighted, "rep", scatter_dimension=0, tiled=True), state)


def solution(mesh):
    placed = (
        P("rep", "gx", "gy", None),
        P("rep", "gx", "gy", None),
        P("rep", "gx", "gy", None),
        P("rep"),
        P("gx", "gy"),
        P(),
    )
    return jax.shard_map(
        local,
        mesh=mesh,
        in_specs=placed,
        out_specs=(P(("gx", "rep"), "gy", None), P("rep", "gx", "gy", None)),
        check_vma=False,
    )
```

profile of v0, /device:TPU:0, one launch (start us, length us, event | category | flops | bytes accessed | tf_op | source)
XLA Modules:
  0.0 200.4 jit_solution(6943174080291104848)
XLA Ops:
  7.2 1.4 fusion.61
  10.6 1.9 select_bitcast_fusion
  12.5 2.0 broadcast_select_fusion
  15.9 3.0 %collective-permute-start.4 = (f32[3,1,32,128]{3,2,1,0:T(8,128)S(1)}, f32[3,1,32,128]{3,2,1,0:T(8,128)S(1)}, u32[]{:S(2)}, u32[]{:S(2)}) collective-permute-start(f32[3,1,32,128]{3,2,1,0:T(8,128)S(1)} %get-tuple-element.32), channel_id=1, source_target_pairs={{0,2},{2,4},{4,6},{1,3},{3,5},{5,7},{8,10},{10,12},{12,14},{9,11},... | collective-permute-start | bytes 147464 | tf_op jit(solution)/shard_map/ppermute | solution.py:20
  21.1 4.9 %collective-permute-start.6 = (f32[3,34,1,128]{3,2,1,0:T(1,128)S(1)}, f32[3,34,1,128]{3,2,1,0:T(1,128)S(1)}, u32[]{:S(2)}, u32[]{:S(2)}) collective-permute-start(f32[3,34,1,128]{3,2,1,0:T(1,128)S(1)} %get-tuple-element.26), channel_id=1, source_target_pairs={{0,1},{2,3},{4,5},{6,7},{8,9},{10,11},{12,13},{14,15},{16,17},{18,... | collective-permute-start | bytes 156680 | tf_op jit(solution)/shard_map/ppermute | solution.py:20
  26.0 62.4 %all-reduce.3.cloned.1.call-done = (bf16[32,32,128]{2,1,0:T(8,128)(2,1)}, bf16[1,32,32,128]{3,2,1,0:T(8,128)(2,1)}, bf16[32,32,128]{2,1,0:T(8,128)(2,1)}, bf16[1...) async-done(((bf16[32,32,128]{2,1,0:T(8,128)(2,1)}, bf16[1,32,32,128]{3,2,1,0:T(8,128)(2,1)}, ...) | async-done | bytes 1572880 | tf_op jit(solution)/shard_map/psum | solution.py:31
  89.2 1.7 collective-permute-start
  90.9 1.3 collective-permute-start.1
  93.4 4.4 %collective-permute-start.8 = (bf16[1,32,128]{2,1,0:T(8,128)(2,1)S(1)}, bf16[1,32,128]{2,1,0:T(8,128)(2,1)S(1)}, u32[]{:S(2)}, u32[]{:S(2)}) collective-permute-start(bf16[1,32,128]{2,1,0:T(8,128)(2,1)S(1)} %get-tuple-element.55), channel_id=1, source_target_pairs={{0,2},{2,4},{4,6},{1,3},{3,5},{5,7},{8,10},{10,12},{12,14},{9,11},... | collective-permute-start | bytes 24584 | tf_op jit(solution)/shard_map/ppermute | solution.py:20
  100.8 4.3 %collective-permute-start.16 = (bf16[1,32,128]{2,1,0:T(8,128)(2,1)S(1)}, bf16[1,32,128]{2,1,0:T(8,128)(2,1)S(1)}, u32[]{:S(2)}, u32[]{:S(2)}) collective-permute-start(bf16[1,32,128]{2,1,0:T(8,128)(2,1)S(1)} %get-tuple-element.53), channel_id=1, source_target_pairs={{0,2},{2,4},{4,6},{1,3},{3,5},{5,7},{8,10},{10,12},{12,14},{9,11},... | collective-permute-start | bytes 24584 | tf_op jit(solution)/shard_map/ppermute | solution.py:20
  105.1 1.3 collective-permute-start.17
  107.8 4.5 %collective-permute-start.2 = (bf16[34,1,128]{2,1,0:T(2,128)(2,1)S(1)}, bf16[34,1,128]{2,1,0:T(2,128)(2,1)S(1)}, u32[]{:S(2)}, u32[]{:S(2)}) collective-permute-start(bf16[34,1,128]{2,1,0:T(2,128)(2,1)S(1)} %get-tuple-element.50), channel_id=1, source_target_pairs={{0,1},{2,3},{4,5},{6,7},{8,9},{10,11},{12,13},{14,15},{16,17},{18,... | collective-permute-start | bytes 26120 | tf_op jit(solution)/shard_map/ppermute | solution.py:20
  112.4 1.3 collective-permute-start.11
  113.8 4.5 %collective-permute-start.10 = (bf16[34,1,128]{2,1,0:T(2,128)(2,1)S(1)}, bf16[34,1,128]{2,1,0:T(2,128)(2,1)S(1)}, u32[]{:S(2)}, u32[]{:S(2)}) collective-permute-start(bf16[34,1,128]{2,1,0:T(2,128)(2,1)S(1)} %get-tuple-element.48), channel_id=1, source_target_pairs={{0,1},{2,3},{4,5},{6,7},{8,9},{10,11},{12,13},{14,15},{16,17},{18,... | collective-permute-start | bytes 26120 | tf_op jit(solution)/shard_map/ppermute | solution.py:20
  120.5 4.5 %collective-permute-start.18 = (bf16[34,1,128]{2,1,0:T(2,128)(2,1)S(1)}, bf16[34,1,128]{2,1,0:T(2,128)(2,1)S(1)}, u32[]{:S(2)}, u32[]{:S(2)}) collective-permute-start(bf16[34,1,128]{2,1,0:T(2,128)(2,1)S(1)} %get-tuple-element.46), channel_id=1, source_target_pairs={{0,1},{2,3},{4,5},{6,7},{8,9},{10,11},{12,13},{14,15},{16,17},{18,... | collective-permute-start | bytes 26120 | tf_op jit(solution)/shard_map/ppermute | solution.py:20
  125.5 3.4 %fusion.31 = f32[3,32,32,128]{3,2,1,0:T(8,128)S(1)} fusion(f32[3,32,32,128]{3,2,1,0:T(8,128)S(1)} %convert_element_type.19, f32[3,34,1,128]{3,2,1,0:T(1,128)S(1)} %collective-permute-done.7, f32[3,1,32,128]{3,2,1,0:T(8,128)S(1)} %collective-permute-done.5, f32[3,1,32,128]{3,2,1,0:T(8,128)S(1)} %collective-permute-done.4, ...), kind=kLoop, calls=%fused_computation.61 | loop fusion | flops 9043968 | bytes 11216896 | tf_op jit(solution)/shard_map/mul | solution.py:55
  130.9 3.2 %collective-permute-start.12 = (f32[3,1,32,128]{3,2,1,0:T(8,128)S(1)}, f32[3,1,32,128]{3,2,1,0:T(8,128)S(1)}, u32[]{:S(2)}, u32[]{:S(2)}) collective-permute-start(f32[3,1,32,128]{3,2,1,0:T(8,128)S(1)} %get-tuple-element.30), channel_id=1, source_target_pairs={{0,2},{2,4},{4,6},{1,3},{3,5},{5,7},{8,10},{10,12},{12,14},{9,11},... | collective-permute-start | bytes 147464 | tf_op jit(solution)/shard_map/ppermute | solution.py:20
  136.3 4.5 %collective-permute-start.14 = (f32[3,34,1,128]{3,2,1,0:T(1,128)S(1)}, f32[3,34,1,128]{3,2,1,0:T(1,128)S(1)}, u32[]{:S(2)}, u32[]{:S(2)}) collective-permute-start(f32[3,34,1,128]{3,2,1,0:T(1,128)S(1)} %get-tuple-element.24), channel_id=1, source_target_pairs={{0,1},{2,3},{4,5},{6,7},{8,9},{10,11},{12,13},{14,15},{16,17},{18,... | collective-permute-start | bytes 156680 | tf_op jit(solution)/shard_map/ppermute | solution.py:20
  141.3 1.3 collective-permute-done.14
  143.1 3.5 %fusion.19 = f32[3,32,32,128]{3,2,1,0:T(8,128)S(1)} fusion(f32[3,32,32,128]{3,2,1,0:T(8,128)S(1)} %fusion.31, f32[3,34,1,128]{3,2,1,0:T(1,128)S(1)} %collective-permute-done.15, f32[3,1,32,128]{3,2,1,0:T(8,128)S(1)} %collective-permute-done.13, f32[3,1,32,128]{3,2,1,0:T(8,128)S(1)} %collective-permute-done.12, ...), kind=kLoop, calls=%fused_computation.37 | loop fusion | flops 9043968 | bytes 11216896 | tf_op jit(solution)/shard_map/mul | solution.py:55
  147.9 5.1 %collective-permute-start.20 = (f32[3,1,32,128]{3,2,1,0:T(8,128)S(1)}, f32[3,1,32,128]{3,2,1,0:T(8,128)S(1)}, u32[]{:S(2)}, u32[]{:S(2)}) collective-permute-start(f32[3,1,32,128]{3,2,1,0:T(8,128)S(1)} %get-tuple-element.28), channel_id=1, source_target_pairs={{0,2},{2,4},{4,6},{1,3},{3,5},{5,7},{8,10},{10,12},{12,14},{9,11},... | collective-permute-start | bytes 147464 | tf_op jit(solution)/shard_map/ppermute | solution.py:20
  155.2 4.7 %collective-permute-start.22 = (f32[3,34,1,128]{3,2,1,0:T(1,128)S(1)}, f32[3,34,1,128]{3,2,1,0:T(1,128)S(1)}, u32[]{:S(2)}, u32[]{:S(2)}) collective-permute-start(f32[3,34,1,128]{3,2,1,0:T(1,128)S(1)} %get-tuple-element.22), channel_id=1, source_target_pairs={{0,1},{2,3},{4,5},{6,7},{8,9},{10,11},{12,13},{14,15},{16,17},{18,... | collective-permute-start | bytes 156680 | tf_op jit(solution)/shard_map/ppermute | solution.py:20
  162.2 5.2 %multiply_reduce_fusion = (f32[32,32,128]{2,1,0:T(8,128)}, f32[3,32,32,128]{3,2,1,0:T(8,128)}) fusion(f32[3]{0:T(128)S(1)} %copy-done.7, f32[3,32,32,128]{3,2,1,0:T(8,128)S(1)} %fusion.19, f32[3,32,32,64]{3,2,1,0:T(8,128)S(1)} %get-tuple-element.11, f32[3,32,32,64]{3,2,1,0:T(8,128)S(1)} %get-tuple-element.10, ...), kind=kLoop, calls=%fused_computation.75 | loop fusion | flops 9699328 | bytes 11741196 | tf_op jit(solution)/shard_map/reduce_sum | solution.py:68
  167.5 26.1 %reduce-scatter.2.cloned.1.call-done = f32[8,32,128]{2,1,0:T(8,128)} async-done(((f32[32,32,128]{2,1,0:T(8,128)}), f32[8,32,128]{2,1,0:T(8,128)}) %reduce-scatter.2.cloned.1.call-update) | async-done | bytes 131088 | tf_op jit(solution)/shard_map/reduce_scatter | solution.py:69
  (96 shorter events, 23.2 us)
Async XLA Ops:
  7.2 81.2 %all-reduce.3.cloned.1.call-start = ((), (), s32[]{:S(2)}) async-start(), calls=%async_computation.2 | async-start | bytes 3145728 | tf_op jit(solution)/shard_map/psum | solution.py:31
  14.5 179.0 %reduce-scatter.2.cloned.1.call-start = ((), (), s32[]{:S(2)}) async-start(), calls=%async_computation.1 | async-start | bytes 655360 | tf_op jit(solution)/shard_map/reduce_scatter | solution.py:69
  14.6 4.6 %collective-permute-start.5 = (f32[3,1,32,128]{3,2,1,0:T(8,128)S(1)}, f32[3,1,32,128]{3,2,1,0:T(8,128)S(1)}, u32[]{:S(2)}, u32[]{:S(2)}) collective-permute-start(f32[3,1,32,128]{3,2,1,0:T(8,128)S(1)} %get-tuple-element.33), channel_id=1, source_target_pairs={{2,0},{4,2},{6,4},{3,1},{5,3},{7,5},{10,8},{12,10},{14,12},{11,9},... | collective-permute-start | bytes 147464 | tf_op jit(solution)/shard_map/ppermute | solution.py:22
  19.8 100.7 %collective-permute-start.7 = (f32[3,34,1,128]{3,2,1,0:T(1,128)S(1)}, f32[3,34,1,128]{3,2,1,0:T(1,128)S(1)}, u32[]{:S(2)}, u32[]{:S(2)}) collective-permute-start(f32[3,34,1,128]{3,2,1,0:T(1,128)S(1)} %get-tuple-element.27), channel_id=1, source_target_pairs={{1,0},{3,2},{5,4},{7,6},{9,8},{11,10},{13,12},{15,14},{17,16},{19,... | collective-permute-start | bytes 156680 | tf_op jit(solution)/shard_map/ppermute | solution.py:22
  21.1 103.9 %collective-permute-start.6 = (f32[3,34,1,128]{3,2,1,0:T(1,128)S(1)}, f32[3,34,1,128]{3,2,1,0:T(1,128)S(1)}, u32[]{:S(2)}, u32[]{:S(2)}) collective-permute-start(f32[3,34,1,128]{3,2,1,0:T(1,128)S(1)} %get-tuple-element.26), channel_id=1, source_target_pairs={{0,1},{2,3},{4,5},{6,7},{8,9},{10,11},{12,13},{14,15},{16,17},{18,... | collective-permute-start | bytes 156680 | tf_op jit(solution)/shard_map/ppermute | solution.py:20
  89.2 10.2 %collective-permute-start = (bf16[1,32,128]{2,1,0:T(8,128)(2,1)S(1)}, bf16[1,32,128]{2,1,0:T(8,128)(2,1)S(1)}, u32[]{:S(2)}, u32[]{:S(2)}) collective-permute-start(bf16[1,32,128]{2,1,0:T(8,128)(2,1)S(1)} %get-tuple-element.57), channel_id=1, source_target_pairs={{0,2},{2,4},{4,6},{1,3},{3,5},{5,7},{8,10},{10,12},{12,14},{9,11},... | collective-permute-start | bytes 24584 | tf_op jit(solution)/shard_map/ppermute | solution.py:20
  90.9 9.9 %collective-permute-start.1 = (bf16[1,32,128]{2,1,0:T(8,128)(2,1)S(1)}, bf16[1,32,128]{2,1,0:T(8,128)(2,1)S(1)}, u32[]{:S(2)}, u32[]{:S(2)}) collective-permute-start(bf16[1,32,128]{2,1,0:T(8,128)(2,1)S(1)} %get-tuple-element.56), channel_id=1, source_target_pairs={{2,0},{4,2},{6,4},{3,1},{5,3},{7,5},{10,8},{12,10},{14,12},{11,9},... | collective-permute-start | bytes 24584 | tf_op jit(solution)/shard_map/ppermute | solution.py:22
  93.4 11.7 %collective-permute-start.8 = (bf16[1,32,128]{2,1,0:T(8,128)(2,1)S(1)}, bf16[1,32,128]{2,1,0:T(8,128)(2,1)S(1)}, u32[]{:S(2)}, u32[]{:S(2)}) collective-permute-start(bf16[1,32,128]{2,1,0:T(8,128)(2,1)S(1)} %get-tuple-element.55), channel_id=1, source_target_pairs={{0,2},{2,4},{4,6},{1,3},{3,5},{5,7},{8,10},{10,12},{12,14},{9,11},... | collective-permute-start | bytes 24584 | tf_op jit(solution)/shard_map/ppermute | solution.py:20
  99.4 7.1 %collective-permute-start.9 = (bf16[1,32,128]{2,1,0:T(8,128)(2,1)S(1)}, bf16[1,32,128]{2,1,0:T(8,128)(2,1)S(1)}, u32[]{:S(2)}, u32[]{:S(2)}) collective-permute-start(bf16[1,32,128]{2,1,0:T(8,128)(2,1)S(1)} %get-tuple-element.54), channel_id=1, source_target_pairs={{2,0},{4,2},{6,4},{3,1},{5,3},{7,5},{10,8},{12,10},{14,12},{11,9},... | collective-permute-start | bytes 24584 | tf_op jit(solution)/shard_map/ppermute | solution.py:22
  100.8 7.1 %collective-permute-start.16 = (bf16[1,32,128]{2,1,0:T(8,128)(2,1)S(1)}, bf16[1,32,128]{2,1,0:T(8,128)(2,1)S(1)}, u32[]{:S(2)}, u32[]{:S(2)}) collective-permute-start(bf16[1,32,128]{2,1,0:T(8,128)(2,1)S(1)} %get-tuple-element.53), channel_id=1, source_target_pairs={{0,2},{2,4},{4,6},{1,3},{3,5},{5,7},{8,10},{10,12},{12,14},{9,11},... | collective-permute-start | bytes 24584 | tf_op jit(solution)/shard_map/ppermute | solution.py:20
  105.1 7.3 %collective-permute-start.17 = (bf16[1,32,128]{2,1,0:T(8,128)(2,1)S(1)}, bf16[1,32,128]{2,1,0:T(8,128)(2,1)S(1)}, u32[]{:S(2)}, u32[]{:S(2)}) collective-permute-start(bf16[1,32,128]{2,1,0:T(8,128)(2,1)S(1)} %get-tuple-element.52), channel_id=1, source_target_pairs={{2,0},{4,2},{6,4},{3,1},{5,3},{7,5},{10,8},{12,10},{14,12},{11,9},... | collective-permute-start | bytes 24584 | tf_op jit(solution)/shard_map/ppermute | solution.py:22
  106.5 7.3 %collective-permute-start.3 = (bf16[34,1,128]{2,1,0:T(2,128)(2,1)S(1)}, bf16[34,1,128]{2,1,0:T(2,128)(2,1)S(1)}, u32[]{:S(2)}, u32[]{:S(2)}) collective-permute-start(bf16[34,1,128]{2,1,0:T(2,128)(2,1)S(1)} %get-tuple-element.51), channel_id=1, source_target_pairs={{1,0},{3,2},{5,4},{7,6},{9,8},{11,10},{13,12},{15,14},{17,16},{19,... | collective-permute-start | bytes 26120 | tf_op jit(solution)/shard_map/ppermute | solution.py:22
  107.8 10.5 %collective-permute-start.2 = (bf16[34,1,128]{2,1,0:T(2,128)(2,1)S(1)}, bf16[34,1,128]{2,1,0:T(2,128)(2,1)S(1)}, u32[]{:S(2)}, u32[]{:S(2)}) collective-permute-start(bf16[34,1,128]{2,1,0:T(2,128)(2,1)S(1)} %get-tuple-element.50), channel_id=1, source_target_pairs={{0,1},{2,3},{4,5},{6,7},{8,9},{10,11},{12,13},{14,15},{16,17},{18,... | collective-permute-start | bytes 26120 | tf_op jit(solution)/shard_map/ppermute | solution.py:20
  112.4 18.4 %collective-permute-start.11 = (bf16[34,1,128]{2,1,0:T(2,128)(2,1)S(1)}, bf16[34,1,128]{2,1,0:T(2,128)(2,1)S(1)}, u32[]{:S(2)}, u32[]{:S(2)}) collective-permute-start(bf16[34,1,128]{2,1,0:T(2,128)(2,1)S(1)} %get-tuple-element.49), channel_id=1, source_target_pairs={{1,0},{3,2},{5,4},{7,6},{9,8},{11,10},{13,12},{15,14},{17,16},{19,... | collective-permute-start | bytes 26120 | tf_op jit(solution)/shard_map/ppermute | solution.py:22
  113.8 20.3 %collective-permute-start.10 = (bf16[34,1,128]{2,1,0:T(2,128)(2,1)S(1)}, bf16[34,1,128]{2,1,0:T(2,128)(2,1)S(1)}, u32[]{:S(2)}, u32[]{:S(2)}) collective-permute-start(bf16[34,1,128]{2,1,0:T(2,128)(2,1)S(1)} %get-tuple-element.48), channel_id=1, source_target_pairs={{0,1},{2,3},{4,5},{6,7},{8,9},{10,11},{12,13},{14,15},{16,17},{18,... | collective-permute-start | bytes 26120 | tf_op jit(solution)/shard_map/ppermute | solution.py:20
  118.4 16.1 %collective-permute-start.19 = (bf16[34,1,128]{2,1,0:T(2,128)(2,1)S(1)}, bf16[34,1,128]{2,1,0:T(2,128)(2,1)S(1)}, u32[]{:S(2)}, u32[]{:S(2)}) collective-permute-start(bf16[34,1,128]{2,1,0:T(2,128)(2,1)S(1)} %get-tuple-element.47), channel_id=1, source_target_pairs={{1,0},{3,2},{5,4},{7,6},{9,8},{11,10},{13,12},{15,14},{17,16},{19,... | collective-permute-start | bytes 26120 | tf_op jit(solution)/shard_map/ppermute | solution.py:22
  120.5 14.0 %collective-permute-start.18 = (bf16[34,1,128]{2,1,0:T(2,128)(2,1)S(1)}, bf16[34,1,128]{2,1,0:T(2,128)(2,1)S(1)}, u32[]{:S(2)}, u32[]{:S(2)}) collective-permute-start(bf16[34,1,128]{2,1,0:T(2,128)(2,1)S(1)} %get-tuple-element.46), channel_id=1, source_target_pairs={{0,1},{2,3},{4,5},{6,7},{8,9},{10,11},{12,13},{14,15},{16,17},{18,... | collective-permute-start | bytes 26120 | tf_op jit(solution)/shard_map/ppermute | solution.py:20
  129.0 6.0 %collective-permute-start.13 = (f32[3,1,32,128]{3,2,1,0:T(8,128)S(1)}, f32[3,1,32,128]{3,2,1,0:T(8,128)S(1)}, u32[]{:S(2)}, u32[]{:S(2)}) collective-permute-start(f32[3,1,32,128]{3,2,1,0:T(8,128)S(1)} %get-tuple-element.31), channel_id=1, source_target_pairs={{2,0},{4,2},{6,4},{3,1},{5,3},{7,5},{10,8},{12,10},{14,12},{11,9},... | collective-permute-start | bytes 147464 | tf_op jit(solution)/shard_map/ppermute | solution.py:22
  135.0 6.3 %collective-permute-start.15 = (f32[3,34,1,128]{3,2,1,0:T(1,128)S(1)}, f32[3,34,1,128]{3,2,1,0:T(1,128)S(1)}, u32[]{:S(2)}, u32[]{:S(2)}) collective-permute-start(f32[3,34,1,128]{3,2,1,0:T(1,128)S(1)} %get-tuple-element.25), channel_id=1, source_target_pairs={{1,0},{3,2},{5,4},{7,6},{9,8},{11,10},{13,12},{15,14},{17,16},{19,... | collective-permute-start | bytes 156680 | tf_op jit(solution)/shard_map/ppermute | solution.py:22
  136.3 6.3 %collective-permute-start.14 = (f32[3,34,1,128]{3,2,1,0:T(1,128)S(1)}, f32[3,34,1,128]{3,2,1,0:T(1,128)S(1)}, u32[]{:S(2)}, u32[]{:S(2)}) collective-permute-start(f32[3,34,1,128]{3,2,1,0:T(1,128)S(1)} %get-tuple-element.24), channel_id=1, source_target_pairs={{0,1},{2,3},{4,5},{6,7},{8,9},{10,11},{12,13},{14,15},{16,17},{18,... | collective-permute-start | bytes 156680 | tf_op jit(solution)/shard_map/ppermute | solution.py:20
  146.6 6.9 %collective-permute-start.21 = (f32[3,1,32,128]{3,2,1,0:T(8,128)S(1)}, f32[3,1,32,128]{3,2,1,0:T(8,128)S(1)}, u32[]{:S(2)}, u32[]{:S(2)}) collective-permute-start(f32[3,1,32,128]{3,2,1,0:T(8,128)S(1)} %get-tuple-element.29), channel_id=1, source_target_pairs={{2,0},{4,2},{6,4},{3,1},{5,3},{7,5},{10,8},{12,10},{14,12},{11,9},... | collective-permute-start | bytes 147464 | tf_op jit(solution)/shard_map/ppermute | solution.py:22
  147.9 6.0 %collective-permute-start.20 = (f32[3,1,32,128]{3,2,1,0:T(8,128)S(1)}, f32[3,1,32,128]{3,2,1,0:T(8,128)S(1)}, u32[]{:S(2)}, u32[]{:S(2)}) collective-permute-start(f32[3,1,32,128]{3,2,1,0:T(8,128)S(1)} %get-tuple-element.28), channel_id=1, source_target_pairs={{0,2},{2,4},{4,6},{1,3},{3,5},{5,7},{8,10},{10,12},{12,14},{9,11},... | collective-permute-start | bytes 147464 | tf_op jit(solution)/shard_map/ppermute | solution.py:20
  153.9 6.6 %collective-permute-start.23 = (f32[3,34,1,128]{3,2,1,0:T(1,128)S(1)}, f32[3,34,1,128]{3,2,1,0:T(1,128)S(1)}, u32[]{:S(2)}, u32[]{:S(2)}) collective-permute-start(f32[3,34,1,128]{3,2,1,0:T(1,128)S(1)} %get-tuple-element.23), channel_id=1, source_target_pairs={{1,0},{3,2},{5,4},{7,6},{9,8},{11,10},{13,12},{15,14},{17,16},{19,... | collective-permute-start | bytes 156680 | tf_op jit(solution)/shard_map/ppermute | solution.py:22
  155.2 6.3 %collective-permute-start.22 = (f32[3,34,1,128]{3,2,1,0:T(1,128)S(1)}, f32[3,34,1,128]{3,2,1,0:T(1,128)S(1)}, u32[]{:S(2)}, u32[]{:S(2)}) collective-permute-start(f32[3,34,1,128]{3,2,1,0:T(1,128)S(1)} %get-tuple-element.22), channel_id=1, source_target_pairs={{0,1},{2,3},{4,5},{6,7},{8,9},{10,11},{12,13},{14,15},{16,17},{18,... | collective-permute-start | bytes 156680 | tf_op jit(solution)/shard_map/ppermute | solution.py:20
  (10 other events, 37.8 us)
Sparse Core Ops, SparseCore 0:
  14.6 73.7 all-reduce.2
  167.6 25.8 reduce-scatter.1
where the time goes:
time: 201 us; the launch traced here: 200 us
  waiting for transfers between devices  91.8 us (46%)
  starting transfers between devices  65.1 us (32%)
  other arithmetic  22.3 us (11%)
  between operations  16.7 us (8%)
  local copies, waits for them, and re-layouts  4.45 us (2%)
    psum x1, waiting for transfers between devices, spread_2(): return lax.psum(jnp.where(mine, x, jnp.zeros_like(x)), axis)  62.4 us
    ppermute x12, starting transfers between devices, extended(): lax.ppermute(tail, axis, [(i, (i + 1) % count) for i in range(ends)])  49.6 us
    reduce_scatter x1, waiting for transfers between devices, local(): lax.psum_scatter(weighted, 'rep', scatter_dimension=0, tiled=True)  26.1 us
    ppermute x12, starting transfers between devices, extended(): lax.ppermute(head, axis, [((i + 1) % count, i) for i in range(ends)])  15.5 us
    mul x2, other arithmetic, advance(): return ocean * (state + time_step * (advect + spread + exchange))  6.9 us
    reduce_sum x1, other arithmetic, local(): weighted = jnp.sum(coefficients[:, None, None, None] * state, axis=0)  5.22 us
  transfers between devices with their start and end apart: 26, of which 6 were waited for; matrix products, arithmetic and copies ran while one was open for 6% of the time, Pallas kernels for 0%

commit v1 on v0

v1 whole, which is shorter than its diff:
```python
import functools

import jax
import jax.numpy as jnp
from jax import lax
from jax.experimental import pallas as pl
from jax.experimental.pallas import tpu as pltpu
from jax.sharding import PartitionSpec as P

MESH = pl.DeviceIdType.MESH
STEPS = 3
F32 = jnp.float32
time_step = 0.1


def kernel(
    sizes, pieces, ahead,
    vel, tra, forcing, coef, mask, levels,
    comb, adj,
    states, up, dn, cu, cv, ct, ocean, wsum, rs_up, rs_dn, xs, xr, ys, yr,
    up_s, up_r, dn_s, dn_r, xs_s, xs_r, ys_s, ys_r, rs_s, rs_r,
):
    n, nx, ny = sizes
    reps, rows, cols, lanes = forcing.shape
    half = lanes // 2
    per = rows // pieces
    share = rows // n
    unit = min(per, share)
    z, x, y = lax.axis_index("rep"), lax.axis_index("gx"), lax.axis_index("gy")

    barrier = pltpu.get_barrier_semaphore()
    links = (("rep", z, n), ("gx", x, nx), ("gy", y, ny))
    for name, at, count in links:
        @pl.when(at > 0)
        def _():
            pl.semaphore_signal(barrier, inc=1, device_id={name: at - 1}, device_id_type=MESH)

        @pl.when(at < count - 1)
        def _():
            pl.semaphore_signal(barrier, inc=1, device_id={name: at + 1}, device_id_type=MESH)

    lane = lax.broadcasted_iota(jnp.int32, (cols, lanes), 1)
    row_of = lax.broadcasted_iota(jnp.int32, (cols, lanes), 0)
    first = lane < half
    eye = lax.broadcasted_iota(jnp.int32, (cols, cols), 0) == lax.broadcasted_iota(jnp.int32, (cols, cols), 1)

    def fill_ocean():
        for r in range(rows):
            line = jnp.where(eye, mask[r : r + 1, :].astype(F32), 0.0)
            ocean[r] = jnp.broadcast_to(jnp.sum(line, axis=1, keepdims=True), (cols, lanes))

    def fill_ends():
        none = jnp.zeros(xr.shape[2:], F32)
        thin = jnp.zeros(yr.shape[2:], F32)
        for k in range(STEPS):
            for side, at, count in ((0, x, 0), (1, x, nx - 1)):
                @pl.when(at == count)
                def _():
                    xr[k, side] = none
            for side, at, count in ((0, y, 0), (1, y, ny - 1)):
                @pl.when(at == count)
                def _():
                    yr[k, side] = thin

    def up_copy(k, c):
        part = up.at[k, pl.ds(c * per, per)]
        return pltpu.make_async_remote_copy(part, part, up_s.at[k, c], up_r.at[k, c], {"rep": jnp.minimum(z + 1, n - 1)}, MESH)

    def dn_copy(k, c):
        part = dn.at[k, pl.ds(c * per, per)]
        return pltpu.make_async_remote_copy(part, part, dn_s.at[k, c], dn_r.at[k, c], {"rep": jnp.maximum(z - 1, 0)}, MESH)

    def x_copy(k, side):
        to = jnp.minimum(x + 1, nx - 1) if side == 0 else jnp.maximum(x - 1, 0)
        return pltpu.make_async_remote_copy(
            xs.at[k, side], xr.at[k, side], xs_s.at[k, side], xs_r.at[k, side], {"gx": to}, MESH)

    def y_copy(k, side, c):
        to = jnp.minimum(y + 1, ny - 1) if side == 0 else jnp.maximum(y - 1, 0)
        part = pl.ds(c * per, per)
        return pltpu.make_async_remote_copy(
            ys.at[k, side, part], yr.at[k, side, part], ys_s.at[k, side, c], ys_r.at[k, side, c], {"gy": to}, MESH)

    def rs_copy(side, u):
        to = jnp.minimum(z + 1, n - 1) if side == 0 else jnp.maximum(z - 1, 0)
        part = pl.ds(u * unit, unit)
        dst = rs_up if side == 0 else rs_dn
        return pltpu.make_async_remote_copy(
            wsum.at[part], dst.at[part], rs_s.at[side, u], rs_r.at[side, u], {"rep": to}, MESH)

    x_sends = (x < nx - 1, x > 0)
    x_gets = (x > 0, x < nx - 1)
    y_sends = (y < ny - 1, y > 0)
    y_gets = (y > 0, y < ny - 1)

    def state(k, rep, r):
        return forcing[rep, r].astype(F32) if k == 0 else states[k - 1, rep, r]

    def forward(i):
        ways = ((up, up_copy, z), (dn, dn_copy, n - 1 - z))
        for buf, copy, hops in ways:
            g = i - ahead * hops
            going = jnp.logical_and(g >= 0, g < STEPS * pieces)

            @pl.when(going)
            def _():
                k, p = lax.div(g, pieces), lax.rem(g, pieces)
                turn, odd = lax.div(p, 2), lax.rem(p, 2)
                c = turn + odd * (pieces - 1 - 2 * turn)
                base = c * per

                @pl.when(hops == 0)
                def _():
                    for r in range(per):
                        buf[k, base + r, 0] = vel[0, base + r]
                        buf[k, base + r, 1] = tra[0, base + r]

                @pl.when(hops > 0)
                def _():
                    copy(k, c).wait_recv()

                @pl.when(jnp.logical_and(hops > 0, hops < n - 1))
                def _():
                    mine = jnp.full((cols, lanes), levels[k], jnp.int32) == z
                    for r in range(per):
                        for part, own in ((0, vel), (1, tra)):
                            got = buf[k, base + r, part].astype(F32)
                            kept = jnp.where(mine, own[0, base + r].astype(F32), got)
                            buf[k, base + r, part] = kept.astype(buf.dtype)

                @pl.when(hops < n - 1)
                def _():
                    copy(k, c).start()

    def unpack(k, c):
        mine = jnp.full((cols, lanes), levels[k], jnp.int32) == z
        below = jnp.full((cols, lanes), levels[k], jnp.int32) < z
        for r in range(c * per, c * per + per):
            speed, tracer = (
                jnp.where(mine, own[0, r].astype(F32),
                          jnp.where(below, up[k, r, part].astype(F32), dn[k, r, part].astype(F32)))
                for part, own in ((0, vel), (1, tra)))
            speed = (0.5 * time_step) * speed
            other = pltpu.roll(speed, half, 1)
            cu[k, r] = jnp.where(first, speed, other)
            cv[k, r] = jnp.where(first, other, speed)
            ct[k, r] = -time_step * tracer

    def flux(k, c):
        for r in range(c * per, c * per + per):
            v_head, v_tail = cv[k, r, 0:1, :], cv[k, r, cols - 1 : cols, :]
            for rep in range(reps):
                s = state(k, rep, r)
                ys[k, 0, r, rep : rep + 1, :] = s[cols - 1 : cols] * (time_step + v_tail)
                ys[k, 1, r, rep : rep + 1, :] = s[0:1] * (time_step - v_head)
        for side in (0, 1):
            @pl.when(y_sends[side])
            def _():
                y_copy(k, side, c).start()
        for side, at, r, sign in ((0, pieces - 1, rows - 1, 1.0), (1, 0, 0, -1.0)):
            if c == at:
                speed = time_step + sign * cu[k, r]
                for rep in range(reps):
                    xs[k, side, rep] = state(k, rep, r) * speed

                @pl.when(x_sends[side])
                def _():
                    x_copy(k, side).start()

    def compute(k, c):
        for side in (0, 1):
            @pl.when(y_gets[side])
            def _():
                y_copy(k, side, c).wait_recv()
        for side, at in ((0, 0), (1, pieces - 1)):
            if c == at:
                @pl.when(x_gets[side])
                def _():
                    x_copy(k, side).wait_recv()
        for r in range(c * per, c * per + per):
            plus = time_step + cv[k, r]
            minus = time_step - cv[k, r]
            trace = ct[k, r]
            sea = ocean[r]
            before = time_step + cu[k, r - 1] if r > 0 else None
            after = time_step - cu[k, r + 1] if r < rows - 1 else None
            total = None
            for rep in range(reps):
                s = state(k, rep, r)
                west = state(k, rep, r - 1) * before if r > 0 else xr[k, 0, rep]
                east = state(k, rep, r + 1) * after if r < rows - 1 else xr[k, 1, rep]
                south = jnp.where(row_of == 0, yr[k, 0, r, rep : rep + 1, :], pltpu.roll(s * plus, 1, 0))
                north = jnp.where(row_of == cols - 1, yr[k, 1, r, rep : rep + 1, :], pltpu.roll(s * minus, cols - 1, 0))
                mixed = trace * s
                mixed = mixed - pltpu.roll(mixed, half, 1)
                new = sea * ((1.0 - 4.0 * time_step) * s + mixed + (west + east) + (south + north))
                if k < STEPS - 1:
                    states[k, rep, r] = new
                else:
                    adj[rep, r] = new
                    term = coef[rep] * new
                    total = term if total is None else total + term
            if k == STEPS - 1:
                wsum[r] = total

    def units_of(c):
        return range(c * per // unit, (c + 1) * per // unit)

    def rs_first(c):
        for u in units_of(c):
            d = u * unit // share
            if d > 0:
                @pl.when(z == 0)
                def _():
                    rs_copy(0, u).start()
            if d < n - 1:
                @pl.when(z == n - 1)
                def _():
                    rs_copy(1, u).start()

    def rs_rest(c):
        for u in units_of(c):
            d = u * unit // share
            part = pl.ds(u * unit, unit)

            @pl.when(jnp.logical_and(z > 0, z < d))
            def _():
                rs_copy(0, u).wait_recv()
                wsum[part] += rs_up[part]
                rs_copy(0, u).start()

            @pl.when(jnp.logical_and(z < n - 1, z > d))
            def _():
                rs_copy(1, u).wait_recv()
                wsum[part] += rs_dn[part]
                rs_copy(1, u).start()

    def rs_last(c):
        for u in units_of(c):
            d = u * unit // share
            part = pl.ds(u * unit, unit)
            here = pl.ds(u * unit - d * share, unit)

            @pl.when(z == d)
            def _():
                if d > 0:
                    rs_copy(0, u).wait_recv()
                if d < n - 1:
                    rs_copy(1, u).wait_recv()
                total = wsum[part]
                if d > 0:
                    total += rs_up[part]
                if d < n - 1:
                    total += rs_dn[part]
                comb[here] = total

    order = []
    for i in range((pieces + 1) // 2):
        order += [i, pieces - 1 - i] if i != pieces - 1 - i else [i]
    ready, have, done = [], set(), set()
    for c in order:
        have.add(c)
        now = [d for d in order if d not in done and all(e in have for e in (d - 1, d, d + 1) if 0 <= e < pieces)]
        done.update(now)
        ready.append(now)

    expected = sum(((at > 0).astype(jnp.int32) + (at < count - 1).astype(jnp.int32)) for _, at, count in links)
    pl.semaphore_wait(barrier, expected)

    schedule = [(k, p) for k in range(STEPS) for p in range(pieces)]
    waiting = []
    lag = ahead * (n - 1)
    for i in range(lag):
        forward(i)
        if i == 0:
            fill_ocean()
            fill_ends()
    for g in range(len(schedule) + 2):
        if g < len(schedule):
            k, p = schedule[g]
            forward(g + lag)
            unpack(k, order[p])
        if g >= 2:
            k, p = schedule[g - 2]
            for c in ready[p]:
                compute(k, c)
                if k == STEPS - 1:
                    rs_first(c)
            if k == STEPS - 1:
                for c in waiting:
                    rs_rest(c)
                waiting = list(ready[p])
        if 1 <= g <= len(schedule):
            k, p = schedule[g - 1]
            flux(k, order[p])
    for c in waiting:
        rs_rest(c)
    for c in order:
        rs_last(c)

    for k in range(STEPS):
        for c in range(pieces):
            @pl.when(z < n - 1)
            def _():
                up_copy(k, c).wait_send()

            @pl.when(z > 0)
            def _():
                dn_copy(k, c).wait_send()

            for side in (0, 1):
                @pl.when(y_sends[side])
                def _():
                    y_copy(k, side, c).wait_send()
        for side in (0, 1):
            @pl.when(x_sends[side])
            def _():
                x_copy(k, side).wait_send()
    for u in range(rows // unit):
        d = u * unit // share

        @pl.when(z < d)
        def _():
            rs_copy(0, u).wait_send()

        @pl.when(z > d)
        def _():
            rs_copy(1, u).wait_send()


def local(sizes, velocity, tracers, forcing, coefficients, land_mask, step_levels):
    n = sizes[0]
    reps, rows, cols, lanes = forcing.shape
    pieces = min(8, rows)
    per, share = rows // pieces, rows // n
    units = rows // min(per, share)
    whole = pl.BlockSpec(memory_space=pltpu.VMEM)
    small = pl.BlockSpec(memory_space=pltpu.SMEM)
    grid = (rows, cols, lanes)
    dma = pltpu.SemaphoreType.DMA
    return pl.pallas_call(
        functools.partial(kernel, sizes, pieces, 2),
        out_shape=(
            jax.ShapeDtypeStruct((share, cols, lanes), F32),
            jax.ShapeDtypeStruct(forcing.shape, F32),
        ),
        in_specs=[whole, whole, whole, small, whole, small],
        out_specs=(whole, whole),
        scratch_shapes=[
            pltpu.VMEM((STEPS - 1, reps) + grid, F32),
            pltpu.VMEM((STEPS, rows, 2, cols, lanes), velocity.dtype),
            pltpu.VMEM((STEPS, rows, 2, cols, lanes), velocity.dtype),
            pltpu.VMEM((STEPS,) + grid, F32),
            pltpu.VMEM((STEPS,) + grid, F32),
            pltpu.VMEM((STEPS,) + grid, F32),
            pltpu.VMEM(grid, F32),
            pltpu.VMEM(grid, F32),
            pltpu.VMEM(grid, F32),
            pltpu.VMEM(grid, F32),
            pltpu.VMEM((STEPS, 2, reps, cols, lanes), F32),
            pltpu.VMEM((STEPS, 2, reps, cols, lanes), F32),
            pltpu.VMEM((STEPS, 2, rows, reps, lanes), F32),
            pltpu.VMEM((STEPS, 2, rows, reps, lanes), F32),
            dma((STEPS, pieces)), dma((STEPS, pieces)),
            dma((STEPS, pieces)), dma((STEPS, pieces)),
            dma((STEPS, 2)), dma((STEPS, 2)),
            dma((STEPS, 2, pieces)), dma((STEPS, 2, pieces)),
            dma((2, units)), dma((2, units)),
        ],
        compiler_params=pltpu.CompilerParams(
            collective_id=0, has_side_effects=True, vmem_limit_bytes=40 * 1024 * 1024
        ),
        cost_estimate=pl.CostEstimate(flops=STEPS * 20 * forcing.size, bytes_accessed=8 * forcing.size, transcendentals=0),
    )(velocity, tracers, forcing, coefficients, land_mask, step_levels)


def solution(mesh):
    placed = (
        P("rep", "gx", "gy", None),
        P("rep", "gx", "gy", None),
        P("rep", "gx", "gy", None),
        P("rep"),
        P("gx", "gy"),
        P(),
    )
    sizes = tuple(mesh.shape[name] for name in ("rep", "gx", "gy"))
    return jax.shard_map(
        functools.partial(local, sizes),
        mesh=mesh,
        in_specs=placed,
        out_specs=(P(("gx", "rep"), "gy", None), P("rep", "gx", "gy", None)),
        check_vma=False,
    )
```

time: 201 us -> 81.5 us (0.41)
  the two profiles are of different devices: /device:TPU:0 before, /device:TPU:8 now
where the time goes in v1:
time: 81.5 us; the launch traced here: 81.2 us
  Pallas kernels  73.7 us (90%)
  local copies, waits for them, and re-layouts  6.85 us (8%)
    pallas_call x1, Pallas kernels, local(): pl.pallas_call(functools.partial(kernel, sizes, pieces, 2), out_shape=(ja...  73.7 us
    unnamed x14, local copies, waits for them, and re-layouts  6.85 us

profile of v1, /device:TPU:8, one launch (start us, length us, event | category | flops | bytes accessed | tf_op | source)
XLA Modules:
  0.0 81.2 jit_solution(9903059314291448539)
XLA Ops:
  0.6 0.0 copy-start
  0.6 1.1 %copy-done = bf16[3,32,32,128]{3,2,1,0:T(8,128)(2,1)S(1)} copy-done((bf16[3,32,32,128]{3,2,1,0:T(8,128)(2,1)S(1)}, bf16[3,32,32,128]{3,2,1,0:T(8,128)(2,1)}, u32[]{:S(2)}) %copy-start) | copy-done | bytes 786456
  1.8 0.0 copy-start.1
  1.8 0.9 %copy-done.1 = bf16[1,32,32,128]{3,2,1,0:T(8,128)(2,1)S(1)} copy-done((bf16[1,32,32,128]{3,2,1,0:T(8,128)(2,1)S(1)}, bf16[1,32,32,128]{3,2,1,0:T(8,128)(2,1)}, u32[]{:S(2)}) %copy-start.1) | copy-done | bytes 262168
  2.7 0.0 copy-start.2
  2.7 0.9 %copy-done.2 = bf16[1,32,32,128]{3,2,1,0:T(8,128)(2,1)S(1)} copy-done((bf16[1,32,32,128]{3,2,1,0:T(8,128)(2,1)S(1)}, bf16[1,32,32,128]{3,2,1,0:T(8,128)(2,1)}, u32[]{:S(2)}) %copy-start.2) | copy-done | bytes 262168
  3.7 0.0 copy-start.3
  3.7 0.7 copy-done.3
  4.4 0.0 copy-start.4
  4.4 0.7 copy-done.4
  5.0 0.0 copy-start.5
  5.0 0.7 copy-done.5
  5.7 73.7 %shard_map.77 = (f32[8,32,128]{2,1,0:T(8,128)S(1)}, f32[3,32,32,128]{3,2,1,0:T(8,128)S(1)}) custom-call(bf16[1,32,32,128]{3,2,1,0:T(8,128)(2,1)S(1)} %copy-done.1, bf16[1,32,32,128]{3,2,1,0:T(8,128)(2,1)S(1)} %copy-done.2, bf16[3,32,32,128]{3,2,1,0:T(8,128)(2,1)S(1)} %copy-done, f32[3]{0:T(128)S(1)} %copy-done.4, s32[32,32]{1,0:T(8,128)S(1)} %copy-done.3, ...), custom_call_target="tpu_custom_call" | custom-call | flops 23592960 | bytes 3145728 | tf_op jit(solution)/shard_map/pallas_call | solution.py:341
  79.4 0.7 copy.10
  80.1 1.1 %copy.11 = f32[3,32,32,128]{3,2,1,0:T(8,128)} copy(f32[3,32,32,128]{3,2,1,0:T(8,128)S(1)} %get-tuple-element.5) | data formatting | bytes 3145728
Async XLA Ops:
  0.6 1.1 %copy-start = (bf16[3,32,32,128]{3,2,1,0:T(8,128)(2,1)S(1)}, bf16[3,32,32,128]{3,2,1,0:T(8,128)(2,1)}, u32[]{:S(2)}) copy-start(bf16[3,32,32,128]{3,2,1,0:T(8,128)(2,1)} %forcing.1) | copy-start | bytes 2359300
  1.8 0.9 %copy-start.1 = (bf16[1,32,32,128]{3,2,1,0:T(8,128)(2,1)S(1)}, bf16[1,32,32,128]{3,2,1,0:T(8,128)(2,1)}, u32[]{:S(2)}) copy-start(bf16[1,32,32,128]{3,2,1,0:T(8,128)(2,1)} %vel.1) | copy-start | bytes 786436
  2.7 0.9 %copy-start.2 = (bf16[1,32,32,128]{3,2,1,0:T(8,128)(2,1)S(1)}, bf16[1,32,32,128]{3,2,1,0:T(8,128)(2,1)}, u32[]{:S(2)}) copy-start(bf16[1,32,32,128]{3,2,1,0:T(8,128)(2,1)} %tra.1) | copy-start | bytes 786436
  3.7 0.7 copy-start.3
  4.4 0.7 copy-start.4
  5.0 0.7 copy-start.5
